TPU v7x, 32 devices: a whole 2x2x4 slice. The times are simulated.
32 devices in a mesh: wave: 2 (over y), gy: 4 (over z), gz: 2 (over x), vec: 2 (over core).
Axes of the slice: x: 2, y: 2, z: 4, core: 2. Of those that a mesh axis runs over, the one named last changes fastest.
Arguments:
- forcing: float32 [8, 8, 512, 1024], P(('wave', 'vec'), None, 'gy', 'gz'), parts along dimension 0, may hold values from -6 to 6
- wavenumber: float32 [2], P('wave'), parts along dimension 0, may hold values from 0.5 to 2
- mean_flow: float32 [9, 512, 1024], P(None, 'gy', 'gz'), may hold values from -3 to 3
- viscosity: float32 [512, 1024], P('gy', 'gz'), may hold values from 0.05 to 0.5
- viscosity_slope: float32 [2, 512, 1024], P(None, 'gy', 'gz'), may hold values from -1.8 to 1.8
Outputs:
- response: float32 [8, 8, 512, 1024], P(('wave', 'vec'), None, 'gy', 'gz'), parts along dimension 0
There are 2 independent parts, one for each index of `wave`. A program takes and returns all parts, laid end to end along the dimension named above; an argument that names none is the same for every part. Nothing has to cross between parts.
All inputs are finite; a program needn't handle non-finite values.
Results may differ from a plain program's by a relative error of at most 0.00005.
Values sent between devices are 32-bit elements; how exact they have to be, the bound alone decides.
A program may use at most 128 MiB of HBM per device.

v0:
```python
import math

import jax
import jax.numpy as jnp
from jax import lax
from jax.sharding import PartitionSpec as P

precise = lax.Precision.HIGHEST


def angle_table(points):
    last_index = points - 1
    row_index = jnp.arange(points, dtype=jnp.int32)[:, None]
    col_index = jnp.arange(points, dtype=jnp.int32)[None, :]
    unit = math.pi / (2.0 * last_index)
    sine_row = jnp.sin(
        2.0 * unit * jnp.minimum(row_index, last_index - row_index).astype(jnp.float32)
    )
    total = row_index + col_index
    half_sum = jnp.sin(unit * jnp.minimum(total, 2 * last_index - total).astype(jnp.float32))
    half_diff = jnp.sin(unit * (row_index - col_index).astype(jnp.float32))
    parity = (1 - 2 * (total % 2)).astype(jnp.float32)
    weight = jnp.where((col_index == 0) | (col_index == last_index), 0.5, 1.0).astype(jnp.float32)
    same = row_index == col_index
    denominator = jnp.where(same, 1.0, 2.0 * half_sum * half_diff)
    offdiag = jnp.where(same, 0.0, math.pi / last_index * sine_row * parity * weight / denominator)
    diagonal = -jnp.sum(offdiag, axis=1)
    return offdiag + jnp.diag(diagonal)


def rotate(values):
    return jnp.stack((-values[..., 1, :, :], values[..., 0, :, :]), axis=-3)


def apply_operator(
    forcing, grad_y, curve_y, grad_z, curve_z, streamwise, mean_flow, viscosity, viscosity_slope
):
    full_shape = forcing.shape
    split_shape = full_shape[:-3] + (4, 2) + full_shape[-2:]
    source = forcing.reshape(split_shape)
    grad_y = grad_y.reshape(split_shape)
    curve_y = curve_y.reshape(split_shape)
    grad_z = grad_z.reshape(split_shape)
    curve_z = curve_z.reshape(split_shape)
    velocity = source[..., :3, :, :, :]
    advection = (
        streamwise * mean_flow[0] * rotate(velocity)
        + mean_flow[1] * grad_y[..., :3, :, :, :]
        + mean_flow[2] * grad_z[..., :3, :, :, :]
    )
    slope_y = jnp.stack((mean_flow[3], mean_flow[5], mean_flow[7]))[:, None]
    slope_z = jnp.stack((mean_flow[4], mean_flow[6], mean_flow[8]))[:, None]
    produce = slope_y * source[..., 1:2, :, :, :] + slope_z * source[..., 2:3, :, :, :]
    diffuse = viscosity * (
        curve_y[..., :3, :, :, :] + curve_z[..., :3, :, :, :] - streamwise * streamwise * velocity
    )
    diffuse = (
        diffuse
        + viscosity_slope[0] * grad_y[..., :3, :, :, :]
        + viscosity_slope[1] * grad_z[..., :3, :, :, :]
    )
    pressure = jnp.stack(
        (
            streamwise * rotate(source[..., 3, :, :, :]),
            grad_y[..., 3, :, :, :],
            grad_z[..., 3, :, :, :],
        ),
        axis=-4,
    )
    momentum = -advection - produce + diffuse - pressure
    continuity = (
        streamwise * rotate(source[..., 0, :, :, :])
        + grad_y[..., 1, :, :, :]
        + grad_z[..., 2, :, :, :]
    )
    action = jnp.concatenate((momentum, continuity[..., None, :, :, :]), axis=-4)
    return action.reshape(full_shape)


def mirror_rows(values):
    groups = lax.axis_size("gy")
    first_pass = lax.all_to_all(values, "gy", split_axis=1, concat_axis=1, tiled=True)
    second_pass = lax.all_to_all(
        jnp.flip(first_pass, 1), "gy", split_axis=1, concat_axis=1, tiled=True
    )
    fields, rows_local, cols_local = second_pass.shape
    blocks = second_pass.reshape(fields, groups, rows_local // groups, cols_local)
    return jnp.flip(blocks, 1).reshape(fields, rows_local, cols_local)


def mirror_cols(values):
    groups = lax.axis_size("gz")
    first_pass = lax.all_to_all(values, "gz", split_axis=2, concat_axis=2, tiled=True)
    second_pass = lax.all_to_all(
        jnp.flip(first_pass, 2), "gz", split_axis=2, concat_axis=2, tiled=True
    )
    fields, rows_local, cols_local = second_pass.shape
    blocks = second_pass.reshape(fields, rows_local, groups, cols_local // groups)
    return jnp.flip(blocks, 2).reshape(fields, rows_local, cols_local)


def shards(forcing, wavenumber, mean_flow, viscosity, viscosity_slope):
    vectors, components, rows_local, cols_local = forcing.shape
    rows_total = rows_local * lax.axis_size("gy")
    cols_total = cols_local * lax.axis_size("gz")
    table_y = angle_table(rows_total)
    table_z = angle_table(cols_total)
    flattened = forcing.reshape(vectors * components, rows_local, cols_local)
    first = jnp.einsum(
        "ij,fjk->fik",
        table_y,
        lax.all_to_all(flattened, "gy", split_axis=0, concat_axis=1, tiled=True),
        precision=precise,
    )
    second = jnp.einsum("ij,fjk->fik", table_y, first, precision=precise)
    grad_y = lax.all_to_all(first, "gy", split_axis=1, concat_axis=0, tiled=True)
    curve_y = lax.all_to_all(second, "gy", split_axis=1, concat_axis=0, tiled=True)
    own_start = lax.axis_index("gz") * cols_local
    own_rows = lax.dynamic_slice_in_dim(table_z, own_start, cols_local, 0)
    own_second = jnp.dot(own_rows, table_z, precision=precise, preferred_element_type=jnp.float32)
    piece = lax.all_gather(flattened, "gz", axis=2, tiled=True)
    grad_z = jnp.einsum("fyj,ij->fyi", piece, own_rows, precision=precise)
    curve_z = jnp.einsum("fyj,ij->fyi", piece, own_second, precision=precise)
    full_shape = forcing.shape
    action = apply_operator(
        forcing,
        grad_y.reshape(full_shape),
        curve_y.reshape(full_shape),
        grad_z.reshape(full_shape),
        curve_z.reshape(full_shape),
        wavenumber[0],
        mean_flow,
        viscosity,
        viscosity_slope,
    )
    y_signs = jnp.array([1.0, 1.0, -1.0, -1.0, 1.0, 1.0, 1.0, 1.0], dtype=jnp.float32)[
        :, None, None
    ]
    z_signs = jnp.array([1.0, 1.0, 1.0, 1.0, -1.0, -1.0, 1.0, 1.0], dtype=jnp.float32)[
        :, None, None
    ]
    flat_shape = (vectors * components, rows_local, cols_local)
    mirrored = mirror_rows(action.reshape(flat_shape)).reshape(full_shape)
    half_y = 0.5 * (action + y_signs * mirrored)
    mirrored = mirror_cols(half_y.reshape(flat_shape)).reshape(full_shape)
    return 0.5 * (half_y + z_signs * mirrored)


def solution(mesh):
    placed = (
        P(("wave", "vec"), None, "gy", "gz"),
        P("wave"),
        P(None, "gy", "gz"),
        P("gy", "gz"),
        P(None, "gy", "gz"),
    )
    return jax.shard_map(
        shards,
        mesh=mesh,
        in_specs=placed,
        out_specs=P(("wave", "vec"), None, "gy", "gz"),
        check_vma=False,
    )
```

profile of v0, /device:TPU:16, one launch (start us, length us, event | category | flops | bytes accessed | tf_op | source)
XLA Modules:
  0.0 780.6 jit_solution(14068977616443532801)
XLA Ops:
  6.5 5.2 all-to-all-start
  11.8 8.3 %fusion.83 = f32[512]{0:T(512)S(1)} fusion(f32[512]{0:T(512)S(1)} %get-tuple-element.33, f32[512]{0:T(512)S(1)} %get-tuple-element.32), kind=kLoop, calls=%fused_computation.111 | loop fusion | flops 8125952 | bytes 6144 | tf_op jit(solution)/shard_map/reduce_sum | solution.py:27
  20.1 81.7 %all-to-all-done = f32[16,128,512]{2,1,0:T(8,128)} async-done(((f32[16,128,512]{2,1,0:T(8,128)}), f32[16,128,512]{2,1,0:T(8,128)}, u32[]{:S(2)}, u32[]{:S(2)}) %all-to-all-start) | async-done | bytes 4194336 | tf_op jit(solution)/shard_map/all_to_all | solution.py:112
  101.8 2.7 copy.85
  104.5 14.8 %convolution_bitcast_fusion.1 = f32[4,512,512]{2,1,0:T(8,128)S(1)} fusion(f32[4,512,512]{2,1,0:T(8,128)S(1)} %bitcast.105, f32[512]{0:T(512)S(1)} %neg.30, f32[512]{0:T(512)S(1)} %get-tuple-element.33, f32[512]{0:T(512)S(1)} %get-tuple-element.32), kind=kOutput, calls=%fused_computation.51 | convolution fusion | flops 6450839552 | bytes 8394752 | tf_op jit(solution)/shard_map/ij,fjk->fik/dot_general | solution.py:109
  119.3 1.9 copy-done.10
  121.3 23.1 %convolution_bitcast_fusion = f32[4,512,512]{1,2,0:T(8,128)} fusion(f32[4,512,512]{2,1,0:T(8,128)S(1)} %convolution_bitcast_fusion.1, f32[512]{0:T(512)S(1)} %neg.30, f32[512]{0:T(512)S(1)} %get-tuple-element.33, f32[512]{0:T(512)S(1)} %get-tuple-element.32), kind=kOutput, calls=%fused_computation.50 | convolution fusion | flops 6450839552 | bytes 8394752 | tf_op jit(solution)/shard_map/ij,fjk->fik/dot_general | solution.py:115
  144.3 5.5 copy.92
  149.9 8.2 %all-to-all-start.2 = ((f32[4,512,512]{2,0,1:T(4,128)}), f32[4,512,512]{2,0,1:T(4,128)}, u32[]{:S(2)}, u32[]{:S(2)}) async-start(f32[4,512,512]{2,0,1:T(4,128)} %copy.92), calls=%async_computation.2 | async-start | bytes 8388608 | tf_op jit(solution)/shard_map/all_to_all | solution.py:117
  158.1 0.5 all-gather.2.cloned.1.call-start
  158.8 4.8 copy.84
  164.3 7.1 copy.86
  171.4 76.0 %all-to-all-done.2 = f32[4,512,512]{2,0,1:T(4,128)} async-done(((f32[4,512,512]{2,0,1:T(4,128)}), f32[4,512,512]{2,0,1:T(4,128)}, u32[]{:S(2)}, u32[]{:S(2)}) %all-to-all-start.2) | async-done | bytes 4194336 | tf_op jit(solution)/shard_map/all_to_all | solution.py:117
  247.4 8.2 %all-to-all-start.1 = ((f32[4,512,512]{2,0,1:T(4,128)}), f32[4,512,512]{2,0,1:T(4,128)}, u32[]{:S(2)}, u32[]{:S(2)}) async-start(f32[4,512,512]{2,0,1:T(4,128)} %copy.86), calls=%async_computation.1 | async-start | bytes 8388608 | tf_op jit(solution)/shard_map/all_to_all | solution.py:116
  255.6 31.7 %fusion.43 = f32[1024]{0:T(1024)S(1)} fusion(f32[1024]{0:T(1024)S(1)} %get-tuple-element.31, f32[1024]{0:T(1024)S(1)} %get-tuple-element.30), kind=kLoop, calls=%fused_computation.56 | loop fusion | flops 32504832 | bytes 12288 | tf_op jit(solution)/shard_map/reduce_sum | solution.py:27
  287.3 4.2 slice_bitcast_fusion.3
  291.6 1.1 maximum_multiply_fusion.1
  292.7 0.8 copy-done.11
  293.5 1.1 multiply_bitcast_fusion
  294.6 1.3 pad_maximum_fusion.1
  295.9 0.9 slice_bitcast_fusion.7
  296.7 1.1 fusion.75
  297.9 2.0 slice_negate_fusion
  299.9 32.9 %fusion.14 = f32[1024,1024]{1,0:T(8,128)S(1)} fusion(f32[1024]{0:T(1024)S(1)} %neg.31, f32[1024]{0:T(1024)S(1)} %get-tuple-element.31, f32[1024]{0:T(1024)S(1)} %get-tuple-element.30), kind=kLoop, calls=%fused_computation.19 | loop fusion | flops 33554432 | bytes 4206592 | tf_op jit(solution)/shard_map/add | solution.py:28
  332.8 2.0 copy-done.7
  334.8 6.9 fusion.49
  341.7 16.1 %fusion.39 = f32[512,16,128]{2,0,1:T(8,128)S(1)} fusion(f32[16,128,1024]{2,1,0:T(8,128)} %all-gather.2.cloned.1.call-done, f32[512,1024]{1,0:T(8,128)S(1)} %fusion.49), kind=kOutput, calls=%fused_computation.52 | convolution fusion | flops 12884901888 | bytes 14680064 | tf_op jit(solution)/shard_map/fyj,ij->fyi/dot_general | solution.py:123
  357.8 1.9 slice.131
  359.7 2.4 copy.114
  362.1 17.0 %fusion.41 = f32[512,16,128]{2,0,1:T(8,128)S(1)} fusion(f32[16,128,1024]{2,1,0:T(8,128)} %all-gather.2.cloned.1.call-done, f32[1024,1024]{1,0:T(8,128)} %copy-done.7, s32[]{:T(128)S(6)} %select_n.84), kind=kOutput, calls=%fused_computation.54 | convolution fusion | flops 12884901888 | bytes 14680068 | tf_op jit(solution)/shard_map/fyj,ij->fyi/dot_general | solution.py:122
  379.1 1.9 copy-done.4
  381.1 1.9 slice.127
  383.0 3.7 copy.112
  386.7 3.1 fusion.115
  389.8 2.6 copy.116
  392.4 2.6 copy.117
  395.0 3.5 copy.93
  398.6 2.7 copy.94
  401.2 3.6 copy.87
  404.9 0.5 copy.88
  405.4 0.7 copy-done.9
  406.1 1.9 fusion.114
  408.0 1.1 copy-done.6
  409.1 1.3 copy-done.1
  410.4 0.4 copy-done.8
  410.8 5.9 fusion.34
  416.7 1.8 pad_maximum_fusion
  418.5 0.6 copy.103
  419.1 1.5 copy-done.3
  420.6 2.4 copy.104
  423.0 94.4 %all_to_all.68 = f32[16,128,512]{2,0,1:T(8,128)} all-to-all(f32[16,128,512]{2,0,1:T(8,128)S(1)} %copy.104), channel_id=1, replica_groups=mesh['wave'=2,'gy'=4,'gz'=2,'vec'=2] {'gy'}, dimensions={1} | all-to-all | bytes 8388608 | tf_op jit(solution)/shard_map/all_to_all | solution.py:82
  517.4 5.0 rev.16
  522.4 8.0 %all-to-all-start.4 = ((f32[16,128,512]{2,0,1:T(8,128)}), f32[16,128,512]{2,0,1:T(8,128)}, u32[]{:S(2)}, u32[]{:S(2)}) async-start(f32[16,128,512]{2,0,1:T(8,128)} %rev.16), calls=%async_computation.4 | async-start | bytes 8388608 | tf_op jit(solution)/shard_map/all_to_all | solution.py:83
  530.5 88.8 %all-to-all-done.4 = f32[16,128,512]{2,0,1:T(8,128)} async-done(((f32[16,128,512]{2,0,1:T(8,128)}), f32[16,128,512]{2,0,1:T(8,128)}, u32[]{:S(2)}, u32[]{:S(2)}) %all-to-all-start.4) | async-done | bytes 4194336 | tf_op jit(solution)/shard_map/all_to_all | solution.py:83
  619.3 6.6 copy.105
  625.9 5.0 rev.17
  631.0 6.7 fusion.25
  637.6 5.5 copy.107
  643.1 54.3 %all_to_all.69 = f32[16,128,512]{1,0,2:T(8,128)} all-to-all(f32[16,128,512]{1,0,2:T(8,128)} %copy.107), channel_id=1, replica_groups=mesh['wave'=2,'gy'=4,'gz'=2,'vec'=2] {'gz'}, dimensions={2} | all-to-all | bytes 8388608 | tf_op jit(solution)/shard_map/all_to_all | solution.py:93
  697.4 4.5 rev.18
  701.9 53.4 %all_to_all.70 = f32[16,128,512]{1,0,2:T(8,128)} all-to-all(f32[16,128,512]{1,0,2:T(8,128)} %rev.18), channel_id=1, replica_groups=mesh['wave'=2,'gy'=4,'gz'=2,'vec'=2] {'gz'}, dimensions={2} | all-to-all | bytes 8388608 | tf_op jit(solution)/shard_map/all_to_all | solution.py:94
  755.3 4.5 rev.19
  759.8 5.3 copy.110
  765.0 8.5 %fusion.28 = f32[2,8,128,512]{3,2,1,0:T(8,128)} fusion(f32[2,8,128,512]{3,2,1,0:T(8,128)} %copy.110, f32[2,8,128,512]{3,2,1,0:T(8,128)} %bitcast.94, f32[8]{0:T(128)S(1)} %copy-done.16, f32[8]{0:T(128)S(1)} %copy-done.15, f32[2,4,2,128,512]{4,3,0,2,1:T(8,128)} %copy-done.3), kind=kLoop, calls=%fused_computation.36 | loop fusion | flops 6291456 | bytes 16777280 | tf_op jit(solution)/shard_map/mul | solution.py:146
  (35 shorter events, 0.6 us)
Async XLA Ops:
  6.5 95.3 %all-to-all-start = ((f32[16,128,512]{2,1,0:T(8,128)}), f32[16,128,512]{2,1,0:T(8,128)}, u32[]{:S(2)}, u32[]{:S(2)}) async-start(f32[16,128,512]{2,1,0:T(8,128)} %bitcast.91), calls=%async_computation | async-start | bytes 8388608 | tf_op jit(solution)/shard_map/all_to_all | solution.py:112
  119.3 2.0 copy-start.10
  149.9 97.5 %all-to-all-start.2 = ((f32[4,512,512]{2,0,1:T(4,128)}), f32[4,512,512]{2,0,1:T(4,128)}, u32[]{:S(2)}, u32[]{:S(2)}) async-start(f32[4,512,512]{2,0,1:T(4,128)} %copy.92), calls=%async_computation.2 | async-start | bytes 8388608 | tf_op jit(solution)/shard_map/all_to_all | solution.py:117
  158.1 183.6 %all-gather.2.cloned.1.call-start = ((), (), s32[]{:S(2)}) async-start(), calls=%async_computation.7 | async-start | bytes 12582912 | tf_op jit(solution)/shard_map/all_gather | solution.py:121
  247.4 153.8 %all-to-all-start.1 = ((f32[4,512,512]{2,0,1:T(4,128)}), f32[4,512,512]{2,0,1:T(4,128)}, u32[]{:S(2)}, u32[]{:S(2)}) async-start(f32[4,512,512]{2,0,1:T(4,128)} %copy.86), calls=%async_computation.1 | async-start | bytes 8388608 | tf_op jit(solution)/shard_map/all_to_all | solution.py:116
  291.5 2.0 copy-start.11
  292.7 3.2 copy-start.14
  294.6 3.3 copy-start
  332.8 2.0 copy-start.7
  379.1 2.0 copy-start.4
  401.2 4.2 copy-start.12
  401.2 4.2 copy-start.13
  404.9 1.2 copy-start.9
  404.9 3.1 copy-start.5
  404.9 4.2 copy-start.6
  405.4 5.0 copy-start.1
  405.4 5.4 copy-start.8
  418.5 2.1 copy-start.3
  420.6 2.4 copy-start.2
  522.4 8.0 %copy-start.15 = (f32[8]{0:T(128)S(1)}, f32[8]{0:T(128)}, u32[]{:S(2)}) copy-start(f32[8]{0:T(128)} %constant.74.clone) | copy-start | bytes 100
  522.4 96.9 %all-to-all-start.4 = ((f32[16,128,512]{2,0,1:T(8,128)}), f32[16,128,512]{2,0,1:T(8,128)}, u32[]{:S(2)}, u32[]{:S(2)}) async-start(f32[16,128,512]{2,0,1:T(8,128)} %rev.16), calls=%async_computation.4 | async-start | bytes 8388608 | tf_op jit(solution)/shard_map/all_to_all | solution.py:83
  759.8 5.3 copy-start.16
Sparse Core Ops, SparseCore 0:
  160.5 104.9 all-gather.1
where the time goes:
time: 794 us; the launch traced here: 781 us
  waiting for transfers between devices  247 us (31%)
  blocking collectives  202 us (25%)
  local copies, waits for them, and re-layouts  105 us (13%)
  other arithmetic  104 us (13%)
  matrix products  77.9 us (10%)
  starting transfers between devices  30 us (4%)
  between operations  14.6 us (2%)
    all_to_all x1, blocking collectives, mirror_rows(): lax.all_to_all(values, 'gy', split_axis=1, concat_axis=1, tiled=True)  94.4 us
    all_to_all x1, waiting for transfers between devices, mirror_rows(): lax.all_to_all(jnp.flip(first_pass, 1), 'gy', split_axis=1, concat_axis=1...  88.8 us
    all_to_all x1, waiting for transfers between devices, shards(): lax.all_to_all(flattened, 'gy', split_axis=0, concat_axis=1, tiled=True)  81.7 us
    all_to_all x1, waiting for transfers between devices, shards(): lax.all_to_all(second, 'gy', split_axis=1, concat_axis=0, tiled=True)  76 us
    all_to_all x1, blocking collectives, mirror_cols(): lax.all_to_all(values, 'gz', split_axis=2, concat_axis=2, tiled=True)  54.3 us
    all_to_all x1, blocking collectives, mirror_cols(): lax.all_to_all(jnp.flip(first_pass, 2), 'gz', split_axis=2, concat_axis=2...  53.4 us
    reduce_sum x2, other arithmetic, angle_table(): diagonal = -jnp.sum(offdiag, axis=1)  40 us
    add x1, other arithmetic, angle_table(): return offdiag + jnp.diag(diagonal)  32.9 us
  transfers between devices with their start and end apart: 5, of which 3 were waited for; matrix products, arithmetic and copies ran while one was open for 21% of the time, Pallas kernels for 0%

commit v1 on v0

--- a/solution.py
+++ b/solution.py
@@ -1,8 +1,11 @@
+import functools
 import math
 
 import jax
 import jax.numpy as jnp
 from jax import lax
+from jax.experimental import pallas as pl
+from jax.experimental.pallas import tpu as pltpu
 from jax.sharding import PartitionSpec as P
 
 precise = lax.Precision.HIGHEST
@@ -146,6 +149,425 @@
     return 0.5 * (half_y + z_signs * mirrored)
 
 
+Y_SIGNS = (1, -1, 1, 1)
+Z_SIGNS = (1, 1, -1, 1)
+SINE_TERMS = 7
+
+
+def short_sine(x):
+    square = x * x
+    total = jnp.full_like(x, 1.0 / math.factorial(2 * SINE_TERMS - 1) * (-1) ** (SINE_TERMS - 1))
+    for k in range(SINE_TERMS - 2, -1, -1):
+        total = total * square + (-1) ** k / math.factorial(2 * k + 1)
+    return total * x
+
+
+def half_rows_of(points, mirrored):
+    half, last_index = points // 2, points - 1
+    row_index = jnp.arange(half, dtype=jnp.int32)[:, None]
+    col_index = jnp.arange(half, dtype=jnp.int32)[None, :]
+    if mirrored:
+        col_index = last_index - col_index
+    unit = math.pi / (2.0 * last_index)
+    sine_row = short_sine(2.0 * unit * row_index.astype(jnp.float32))
+    total = row_index + col_index
+    half_sum = short_sine(unit * jnp.minimum(total, 2 * last_index - total).astype(jnp.float32))
+    half_diff = short_sine(unit * (row_index - col_index).astype(jnp.float32))
+    parity = (1 - 2 * (total % 2)).astype(jnp.float32)
+    weight = jnp.where((col_index == 0) | (col_index == last_index), 0.5, 1.0).astype(jnp.float32)
+    same = row_index == col_index
+    denominator = jnp.where(same, 1.0, 2.0 * half_sum * half_diff)
+    return jnp.where(same, 0.0, math.pi / last_index * sine_row * parity * weight / denominator)
+
+
+def parity_tables(points):
+    near, far = half_rows_of(points, False), half_rows_of(points, True)
+    near = near - jnp.diag(jnp.sum(near, axis=1) + jnp.sum(far, axis=1))
+    even, odd = near + far, near - far
+    second_even = jnp.dot(odd, even, precision=precise)
+    second_odd = jnp.dot(even, odd, precision=precise)
+    return even, odd, second_even, second_odd
+
+
+def split2(x):
+    high = x.astype(jnp.bfloat16)
+    return high, (x - high.astype(jnp.float32)).astype(jnp.bfloat16)
+
+
+def mxu(a, b):
+    return jnp.dot(a, b, preferred_element_type=jnp.float32)
+
+
+def dot3(a, b):
+    a_high, a_low = split2(a)
+    b_high, b_low = split2(b)
+    return mxu(a_high, b_high) + (mxu(a_high, b_low) + mxu(a_low, b_high))
+
+
+def exchange(size):
+    i = lax.broadcasted_iota(jnp.int32, (size, size), 0)
+    j = lax.broadcasted_iota(jnp.int32, (size, size), 1)
+    return jnp.where(i + j == size - 1, 1.0, 0.0).astype(jnp.bfloat16)
+
+
+def split3(x):
+    high, rest = split2(x)
+    middle = x - high.astype(jnp.float32)
+    low = (middle - rest.astype(jnp.float32)).astype(jnp.bfloat16)
+    return high, rest, low
+
+
+def flip_lanes(x):
+    width = x.shape[1]
+    size = 256 if width % 256 == 0 else 128
+    turn = exchange(size)
+    out = []
+    for start in range(width - size, -1, -size):
+        high, middle, low = split3(x[:, start : start + size])
+        out.append(mxu(high, turn) + (mxu(middle, turn) + mxu(low, turn)))
+    return out[0] if len(out) == 1 else jnp.concatenate(out, axis=1)
+
+
+def flip_rows(x):
+    high, middle, low = split3(x)
+    turn = exchange(x.shape[0])
+    return mxu(turn, high) + (mxu(turn, middle) + mxu(turn, low))
+
+
+def times_i(pair):
+    return jnp.concatenate((-pair[1:2], pair[0:1]))
+
+
+def action_along_z(source, grad, curve, streamwise, coefs):
+    u, v, w, p = source
+    stream, advect, uy, uz, vy, vz, wy, wz, nu = (coefs[k : k + 1] for k in range(9))
+    out = []
+    for k, (c, sy, sz) in enumerate(((u, uy, uz), (v, vy, vz), (w, wy, wz))):
+        term = (
+            advect * grad[k]
+            - (streamwise * stream) * times_i(c)
+            - (sy * v + sz * w)
+            + nu * (curve[k] - streamwise * streamwise * c)
+        )
+        if k == 0:
+            term = term - streamwise * times_i(p)
+        if k == 2:
+            term = term - grad[3]
+        out.append(term)
+    out.append(streamwise * times_i(u) + grad[2])
+    return out
+
+
+def body(
+    groups, wave_ref, f_ref, c_ref, tz_ref, ty_ref, out_ref,
+    pair, coef, far, far_coef, lines, line_coef, grad, curve, z_part, z_lines, whole, piece, outgoing,
+    local, cross_s, cross_r, coef_s, coef_r, own_s, own_r, fwd_s, fwd_r, lc_s, lc_r,
+    zp_s, zp_r, q_s, q_r, fin_s, fin_r,
+):
+    rows, cols = f_ref.shape[2], f_ref.shape[3]
+    width = cols // groups
+    half = rows * groups // 2
+    g, h, core = lax.axis_index("gy"), lax.axis_index("gz"), lax.axis_index("vec")
+    streamwise = wave_ref[0]
+    peers = [lax.rem(g + d, groups) for d in range(groups)]
+
+    barrier = pltpu.get_barrier_semaphore()
+    for d in range(1, groups):
+        pl.semaphore_signal(
+            barrier, inc=1, device_id={"gy": peers[d]}, device_id_type=pl.DeviceIdType.MESH
+        )
+    pl.semaphore_signal(barrier, inc=1, device_id={"gz": 1 - h}, device_id_type=pl.DeviceIdType.MESH)
+    pl.semaphore_signal(
+        barrier, inc=1, device_id={"vec": 1 - core}, device_id_type=pl.DeviceIdType.MESH
+    )
+    pl.semaphore_wait(barrier, groups + 1)
+
+    def remote(src, dst, send, recv, device):
+        copy = pltpu.make_async_remote_copy(
+            src_ref=src, dst_ref=dst, send_sem=send, recv_sem=recv,
+            device_id=device, device_id_type=pl.DeviceIdType.MESH,
+        )
+        copy.start()
+        return copy
+
+    def here(src, dst, k):
+        copy = pltpu.make_async_copy(src, dst, local.at[k])
+        copy.start()
+        return copy
+
+    def block(p):
+        return pl.ds(pl.multiple_of(p * width, width), width)
+
+    def block_of(side, p):
+        return block(jnp.where(side == 0, p, groups - 1 - p))
+
+    my_rows = pl.ds(pl.multiple_of(g * rows, rows), rows)
+
+    cross = [
+        remote(
+            f_ref.at[1 - h, pl.ds(2 * k, 2)], pair.at[h, pl.ds(2 * k, 2)],
+            cross_s.at[k], cross_r.at[k], {"gz": 1 - h},
+        )
+        for k in range(4)
+    ]
+    own_lines = [
+        remote(
+            f_ref.at[h, :, :, block_of(h, peers[d])], lines.at[h, :, my_rows, :],
+            own_s.at[d], own_r.at[d], {"gy": peers[d]},
+        )
+        for d in range(1, groups)
+    ]
+    share = c_ref.shape[0] // 2
+    shared = pl.ds(core * share, share)
+    coef_cross = remote(
+        c_ref.at[shared], coef.at[h, shared], coef_s.at[0], coef_r.at[0], {"gz": 1 - h}
+    )
+    own_copy = here(f_ref.at[h], pair.at[h], 0)
+    coef_copy = here(c_ref, coef.at[h], 1)
+    line_copy = here(f_ref.at[h, :, :, block_of(h, g)], lines.at[h, :, my_rows, :], 2)
+    own_copy.wait()
+    forwarded, line_copies = [], [line_copy]
+
+    def derive(k):
+        near = pair[0, 2 * k : 2 * k + 2].reshape(2 * rows, cols)
+        mirror = flip_lanes(pair[1, 2 * k : 2 * k + 2].reshape(2 * rows, cols))
+        far[2 * k : 2 * k + 2] = mirror.reshape(2, rows, cols)
+        even, odd = 0.5 * (near + mirror), 0.5 * (near - mirror)
+        first, second = dot3(even, tz_ref[0]), dot3(odd, tz_ref[1])
+        grad[0, 2 * k : 2 * k + 2] = (second + first).reshape(2, rows, cols)
+        grad[1, 2 * k : 2 * k + 2] = (second - first).reshape(2, rows, cols)
+        if k < 3:
+            first, second = dot3(even, tz_ref[2]), dot3(odd, tz_ref[3])
+            curve[0, 2 * k : 2 * k + 2] = (first + second).reshape(2, rows, cols)
+            curve[1, 2 * k : 2 * k + 2] = (first - second).reshape(2, rows, cols)
+
+    for k in range(4):
+        two = pl.ds(2 * k, 2)
+        cross[k].wait_recv()
+        for d in range(1, groups):
+            forwarded.append(
+                remote(
+                    pair.at[1 - h, two, :, block_of(1 - h, peers[d])],
+                    lines.at[1 - h, two, my_rows, :],
+                    fwd_s.at[k, d], fwd_r.at[k, d], {"gy": peers[d]},
+                )
+            )
+        line_copies.append(
+            here(
+                pair.at[1 - h, two, :, block_of(1 - h, g)],
+                lines.at[1 - h, two, my_rows, :],
+                3 + k,
+            )
+        )
+        derive(k)
+
+    coef_copy.wait()
+    coef_cross.wait_recv()
+    coef_mate = remote(
+        coef.at[1 - h, shared], coef.at[1 - h, shared], coef_s.at[1], coef_r.at[1], {"vec": 1 - core}
+    )
+    coef_mate.wait_recv()
+    coef_lines = []
+    for s in range(2):
+        for d in range(1, groups):
+            coef_lines.append(
+                remote(
+                    coef.at[s, pl.ds(8, 2), :, block_of(s, peers[d])],
+                    line_coef.at[s, :, my_rows, :],
+                    lc_s.at[s, d], lc_r.at[s, d], {"gy": peers[d]},
+                )
+            )
+        line_copies.append(
+            here(coef.at[s, pl.ds(8, 2), :, block_of(s, g)], line_coef.at[s, :, my_rows, :], 7 + s)
+        )
+    for k in range(9):
+        far_coef[k] = flip_lanes(coef[1, k])
+
+    @pl.loop(0, rows // 8)
+    def _(step):
+        at = pl.ds(pl.multiple_of(step * 8, 8), 8)
+
+        def act(source, side, coefs):
+            return action_along_z(
+                [source[2 * k : 2 * k + 2, at, :] for k in range(4)],
+                [grad[side, 2 * k : 2 * k + 2, at, :] for k in range(4)],
+                [curve[side, 2 * k : 2 * k + 2, at, :] for k in range(3)],
+                streamwise,
+                coefs,
+            )
+
+        near_action = act(pair.at[0], 0, coef[0, 0:9, at, :])
+        far_action = act(far, 1, far_coef[0:9, at, :])
+        for k in range(4):
+            z_part[2 * k : 2 * k + 2, at, :] = 0.5 * (near_action[k] + Z_SIGNS[k] * far_action[k])
+
+    z_moves = [
+        remote(
+            z_part.at[:, :, block(peers[d])], z_lines.at[:, my_rows, :],
+            zp_s.at[d], zp_r.at[d], {"gy": peers[d]},
+        )
+        for d in range(1, groups)
+    ]
+    z_copy = here(z_part.at[:, :, block(g)], z_lines.at[:, my_rows, :], 9)
+
+    for copy in line_copies:
+        copy.wait()
+    for copy in own_lines + forwarded + coef_lines:
+        copy.wait_recv()
+
+    def join(values):
+        return jnp.concatenate((values[0], values[1]), axis=1)
+
+    for s in range(2):
+        top_advect, top_nu = line_coef[s, 1, :half], line_coef[s, 0, :half]
+        low = flip_rows(jnp.concatenate((line_coef[s, 0, half:], line_coef[s, 1, half:]), axis=1))
+        low_nu, low_advect = low[:, :width], low[:, width:]
+        top_advect, top_nu, low_advect, low_nu = (
+            jnp.concatenate((x, x), axis=1) for x in (top_advect, top_nu, low_advect, low_nu)
+        )
+
+        def add(k, value, start):
+            value = value if s == 0 else Z_SIGNS[k] * flip_lanes_each(value)
+            for part in range(2):
+                term = 0.5 * value[:, part * width : (part + 1) * width]
+                if start:
+                    whole[2 * k + part, :half] = term
+                else:
+                    whole[2 * k + part, :half] = whole[2 * k + part, :half] + term
+
+        def flip_lanes_each(value):
+            return jnp.concatenate(
+                (flip_lanes(value[:, :width]), flip_lanes(value[:, width:])), axis=1
+            )
+
+        for k in range(4):
+            top = join(lines[s, 2 * k : 2 * k + 2, :half, :])
+            bottom = flip_rows(join(lines[s, 2 * k : 2 * k + 2, half:, :]))
+            even, odd = 0.5 * (top + bottom), 0.5 * (top - bottom)
+            first, second = dot3(ty_ref[0], even), dot3(ty_ref[1], odd)
+            grad_top, grad_low = second + first, second - first
+            if k < 3:
+                first, second = dot3(ty_ref[2], even), dot3(ty_ref[3], odd)
+                top_action = top_advect * grad_top + top_nu * (first + second)
+                low_action = low_advect * grad_low + low_nu * (first - second)
+                add(k, 0.5 * (top_action + Y_SIGNS[k] * low_action), s == 0)
+            if k == 1:
+                add(3, 0.5 * (grad_top + Y_SIGNS[3] * grad_low), s == 0)
+            if k == 3:
+                add(1, -0.5 * (grad_top + Y_SIGNS[1] * grad_low), False)
+
+    z_copy.wait()
+    for copy in z_moves:
+        copy.wait_recv()
+    for k in range(4):
+        top = join(z_lines[2 * k : 2 * k + 2, :half, :])
+        bottom = flip_rows(join(z_lines[2 * k : 2 * k + 2, half:, :]))
+        quarter = join(whole[2 * k : 2 * k + 2, :half, :]) + 0.5 * (top + Y_SIGNS[k] * bottom)
+        mirror = Y_SIGNS[k] * flip_rows(quarter)
+        for part in range(2):
+            whole[2 * k + part, :half] = quarter[:, part * width : (part + 1) * width]
+            whole[2 * k + part, half:] = mirror[:, part * width : (part + 1) * width]
+
+    results = [None]
+    for d in range(1, groups):
+        to_rows = pl.ds(pl.multiple_of(peers[d] * rows, rows), rows)
+        results.append(
+            remote(
+                whole.at[:, to_rows, :], piece.at[d], q_s.at[d], q_r.at[d], {"gy": peers[d]}
+            )
+        )
+    finals = []
+    for d in range(groups):
+        if d:
+            results[d].wait_recv()
+        owner = lax.rem(g - d + groups, groups)
+        flat = (whole[:, my_rows, :] if d == 0 else piece[d]).reshape(8 * rows, width)
+        mirror = flip_lanes(flat)
+        flat, mirror = flat.reshape(8, rows, width), mirror.reshape(8, rows, width)
+        mirror = jnp.concatenate((mirror[:4], -mirror[4:6], mirror[6:]))
+        out_ref[h, :, :, block_of(h, owner)] = jnp.where(h == 0, flat, mirror)
+        outgoing[d] = jnp.where(h == 0, mirror, flat)
+        finals.append(
+            remote(
+                outgoing.at[d], out_ref.at[h, :, :, block_of(1 - h, owner)],
+                fin_s.at[d], fin_r.at[d], {"gz": 1 - h},
+            )
+        )
+    for copy in finals:
+        copy.wait_recv()
+    for copy in cross + own_lines + [coef_cross, coef_mate] + forwarded + coef_lines + z_moves:
+        copy.wait_send()
+    for copy in results[1:] + finals:
+        copy.wait_send()
+
+
+def paired_shards(groups, forcing, wavenumber, mean_flow, viscosity, viscosity_slope):
+    vectors, components, rows, cols = forcing.shape
+    width, rows_total = cols // groups, rows * groups
+    coefs = jnp.concatenate(
+        (
+            mean_flow[0:1],
+            viscosity_slope[1:2] - mean_flow[2:3],
+            mean_flow[3:9],
+            viscosity[None],
+            viscosity_slope[0:1] - mean_flow[1:2],
+        )
+    )
+    tables_z = jnp.stack([table.T for table in parity_tables(2 * cols)])
+    tables_y = jnp.stack(parity_tables(rows_total))
+    f32 = jnp.float32
+    dma = pltpu.SemaphoreType.DMA
+    vmem = pl.BlockSpec(memory_space=pltpu.VMEM)
+    anywhere = pl.BlockSpec(memory_space=pl.ANY)
+    return pl.pallas_call(
+        functools.partial(body, groups),
+        out_shape=jax.ShapeDtypeStruct(forcing.shape, f32),
+        in_specs=[pl.BlockSpec(memory_space=pltpu.SMEM), anywhere, anywhere, vmem, vmem],
+        out_specs=vmem,
+        scratch_shapes=[
+            pltpu.VMEM((2, 8, rows, cols), f32),
+            pltpu.VMEM((2, 10, rows, cols), f32),
+            pltpu.VMEM((8, rows, cols), f32),
+            pltpu.VMEM((9, rows, cols), f32),
+            pltpu.VMEM((2, 8, rows_total, width), f32),
+            pltpu.VMEM((2, 2, rows_total, width), f32),
+            pltpu.VMEM((2, 8, rows, cols), f32),
+            pltpu.VMEM((2, 6, rows, cols), f32),
+            pltpu.VMEM((8, rows, cols), f32),
+            pltpu.VMEM((8, rows_total, width), f32),
+            pltpu.VMEM((8, rows_total, width), f32),
+            pltpu.VMEM((groups, 8, rows, width), f32),
+            pltpu.VMEM((groups, 8, rows, width), f32),
+            dma((10,)),
+            dma((4,)), dma((4,)),
+            dma((2,)), dma((2,)),
+            dma((groups,)), dma((groups,)),
+            dma((4, groups)), dma((4, groups)),
+            dma((2, groups)), dma((2, groups)),
+            dma((groups,)), dma((groups,)),
+            dma((groups,)), dma((groups,)),
+            dma((groups,)), dma((groups,)),
+        ],
+        compiler_params=pltpu.CompilerParams(
+            collective_id=0, has_side_effects=True, vmem_limit_bytes=60 * 1024 * 1024
+        ),
+    )(wavenumber, forcing, coefs, tables_z, tables_y)
+
+
+def shards_of(mesh):
+    groups = mesh.shape["gy"]
+
+    def run(forcing, *others):
+        vectors, _, rows, cols = forcing.shape
+        fits = mesh.shape["gz"] == 2 and mesh.shape["vec"] == 2 and vectors == 2
+        fits = fits and groups % 2 == 0 and groups <= 4
+        if fits and cols == groups * 128 and rows % 16 == 0 and rows * groups <= 512:
+            return paired_shards(groups, forcing, *others)
+        return shards(forcing, *others)
+
+    return run
+
+
 def solution(mesh):
     placed = (
         P(("wave", "vec"), None, "gy", "gz"),
@@ -155,7 +577,7 @@
         P(None, "gy", "gz"),
     )
     return jax.shard_map(
-        shards,
+        shards_of(mesh),
         mesh=mesh,
         in_specs=placed,
         out_specs=P(("wave", "vec"), None, "gy", "gz"),

time: 794 us -> 287 us (0.36); the launches traced: 781 us -> 284 us
  waiting for transfers between devices: 247 us -> 0 us
  Pallas kernels: 0 us -> 238 us
  blocking collectives: 202 us -> 0 us
  local copies, waits for them, and re-layouts: 105 us -> 7.29 us
  other arithmetic: 104 us -> 14.5 us
  matrix products: 77.9 us -> 23.2 us
  starting transfers between devices: 30 us -> 0 us
  between operations: 14.6 us -> 1.24 us
    all_to_all x4 -> x0, waiting for transfers between devices: 246 us -> none  [the longest x1 88.8 us: mirror_rows(): lax.all_to_all(jnp.flip(first_pass, 1), 'gy', split_axis=1, concat_axis=1...]
    pallas_call x0 -> x1, Pallas kernels: none -> 238 us  [paired_shards(): pl.pallas_call(functools.partial(body, groups), out_shape=jax.ShapeDtypeS...]
    all_to_all x3 -> x0, blocking collectives: 202 us -> none  [the longest x1 94.4 us: mirror_rows(): lax.all_to_all(values, 'gy', split_axis=1, concat_axis=1, tiled=True)]
    dot_general x5 -> x4, matrix products: 77.9 us -> 23.2 us  [the longest x2 11.6 us: parity_tables(): second_even = jnp.dot(odd, even, precision=precise)]
    reduce_sum x2, other arithmetic: 40 us -> 6.04 us  [parity_tables(): near = near - jnp.diag(jnp.sum(near, axis=1) + jnp.sum(far, axis=1))]
    all_to_all x4 -> x0, starting transfers between devices: 29.6 us -> none  [the longest x1 8.23 us: shards(): lax.all_to_all(second, 'gy', split_axis=1, concat_axis=0, tiled=True)]
    add x1 -> x4, other arithmetic: 32.9 us -> 4.84 us  [the longest x2 4.83 us: parity_tables(): even, odd = (near + far, near - far)]
    unnamed x39 -> x12, local copies, waits for them, and re-layouts: 27.9 us -> 7.29 us
  transfers between devices with their start and end apart: 5 -> 0, of which waited for: 3 -> 0; matrix products, arithmetic and copies ran while one was open for 21% -> 0% of each run, Pallas kernels for 0% -> 0%
where the time goes in v1:
time: 287 us; the launch traced here: 284 us
  Pallas kernels  238 us (83%)
  matrix products  23.2 us (8%)
  other arithmetic  14.5 us (5%)
  local copies, waits for them, and re-layouts  7.29 us (3%)
    pallas_call x1, Pallas kernels, paired_shards(): pl.pallas_call(functools.partial(body, groups), out_shape=jax.ShapeDtypeS...  238 us
    dot_general x2, matrix products, parity_tables(): second_even = jnp.dot(odd, even, precision=precise)  11.6 us
    dot_general x2, matrix products, parity_tables(): second_odd = jnp.dot(even, odd, precision=precise)  11.6 us
    unnamed x12, local copies, waits for them, and re-layouts  7.29 us
    reduce_sum x2, other arithmetic, parity_tables(): near = near - jnp.diag(jnp.sum(near, axis=1) + jnp.sum(far, axis=1))  6.04 us

profile of v1, /device:TPU:16, one launch (start us, length us, event | category | flops | bytes accessed | tf_op | source)
XLA Modules:
  0.0 284.2 jit_solution(14816921048313012381)
XLA Ops:
  0.7 1.0 fusion.295
  1.8 5.0 %fusion.154 = (f32[512]{0:T(512)S(1)}, f32[512]{0:T(512)S(1)}) fusion(f32[512]{0:T(512)S(1)} %or_select_fusion.2, f32[512]{0:T(512)S(1)} %get-tuple-element.13, s32[512]{0:T(512)S(1)} %iota_subtract_fusion.4, f32[512]{0:T(512)S(1)} %get-tuple-element.14), kind=kLoop, calls=%fused_computation.205 | loop fusion | flops 30931968 | bytes 12288 | tf_op jit(solution)/shard_map/reduce_sum | solution.py:185
  6.8 1.9 convolution_bitcast_fusion.2
  8.7 1.9 convolution_bitcast_fusion.3
  10.7 1.0 fusion.301
  11.6 1.0 pad_maximum_fusion.1.ty_ref
  12.7 9.6 %convolution_bitcast_fusion = f32[1,512,512]{2,1,0:T(8,128)S(1)} fusion(f32[512]{0:T(512)S(1)} %add.1571, f32[512]{0:T(512)S(1)} %get-tuple-element.14, f32[512]{0:T(512)S(1)} %get-tuple-element.13, f32[512]{0:T(512)S(1)} %or_select_fusion.2, s32[512]{0:T(512)S(1)} %iota_subtract_fusion.4), kind=kOutput, calls=%fused_computation.33 | convolution fusion | flops 1673003008 | bytes 1058816 | tf_op jit(solution)/shard_map/dot_general | solution.py:188
  22.3 9.7 %convolution_bitcast_fusion.1 = f32[1,512,512]{2,1,0:T(8,128)S(1)} fusion(f32[512]{0:T(512)S(1)} %add.1571, f32[512]{0:T(512)S(1)} %get-tuple-element.14, f32[512]{0:T(512)S(1)} %get-tuple-element.13, f32[512]{0:T(512)S(1)} %or_select_fusion.2, s32[512]{0:T(512)S(1)} %iota_subtract_fusion.4), kind=kOutput, calls=%fused_computation.34 | convolution fusion | flops 1673003008 | bytes 1058816 | tf_op jit(solution)/shard_map/dot_general | solution.py:187
  32.0 3.9 %fusion.160 = (f32[1,512,512]{2,1,0:T(8,128)S(1)}, f32[1,512,512]{2,1,0:T(8,128)S(1)}) fusion(f32[512]{0:T(512)S(1)} %or_select_fusion.2, f32[512]{0:T(512)S(1)} %get-tuple-element.13, s32[512]{0:T(512)S(1)} %iota_subtract_fusion.4, f32[512]{0:T(512)S(1)} %add.1571, f32[512]{0:T(512)S(1)} %get-tuple-element.14), kind=kLoop, calls=%fused_computation.207 | loop fusion | flops 31457280 | bytes 2107392 | tf_op jit(solution)/shard_map/add | solution.py:186
  35.9 0.0 copy-start.1
  35.9 0.0 copy-start.2
  35.9 2.5 pad_maximum_fusion.tz_ref
  38.4 0.0 copy-done.1
  38.4 0.0 copy-start.3
  38.4 0.2 copy-done.2
  38.7 0.1 slice_dynamic-update-slice_fusion
  38.8 0.6 copy-done.3
  39.5 0.0 copy-start
  39.5 1.5 copy-done
  41.0 238.0 %shard_map.55 = f32[2,8,128,512]{3,2,1,0:T(8,128)} custom-call(f32[1]{0:T(128)S(6)} %copy.11.wave_ref, f32[2,8,128,512]{3,2,1,0:T(8,128)} %f_ref.1, f32[10,128,512]{2,1,0:T(8,128)} %copy-done, f32[4,512,512]{2,1,0:T(8,128)} %pad_maximum_fusion.tz_ref, f32[4,256,256]{2,1,0:T(8,128)} %pad_maximum_fusion.1.ty_ref), custom_call_target="tpu_custom_call" | custom-call | tf_op jit(solution)/shard_map/pallas_call | solution.py:522
  278.9 4.8 %copy.12 = f32[2,8,128,512]{3,2,1,0:T(8,128)} copy(f32[2,8,128,512]{3,2,1,0:T(8,128)} %shard_map.55) | data formatting | bytes 8388608
  (12 shorter events, 0.2 us)
Async XLA Ops:
  35.9 2.5 copy-start.1
  35.9 2.7 copy-start.2
  38.4 1.0 copy-start.3
  39.5 1.5 copy-start

commit v2 on v1

--- a/solution.py
+++ b/solution.py
@@ -162,31 +162,52 @@
     return total * x
 
 
-def half_rows_of(points, mirrored):
-    half, last_index = points // 2, points - 1
-    row_index = jnp.arange(half, dtype=jnp.int32)[:, None]
-    col_index = jnp.arange(half, dtype=jnp.int32)[None, :]
-    if mirrored:
-        col_index = last_index - col_index
+def off_diagonal(points, row_index, col_index):
+    last_index = points - 1
     unit = math.pi / (2.0 * last_index)
     sine_row = short_sine(2.0 * unit * row_index.astype(jnp.float32))
     total = row_index + col_index
     half_sum = short_sine(unit * jnp.minimum(total, 2 * last_index - total).astype(jnp.float32))
     half_diff = short_sine(unit * (row_index - col_index).astype(jnp.float32))
-    parity = (1 - 2 * (total % 2)).astype(jnp.float32)
-    weight = jnp.where((col_index == 0) | (col_index == last_index), 0.5, 1.0).astype(jnp.float32)
+    parity = (1 - 2 * (total & 1)).astype(jnp.float32)
+    weight = jnp.where((col_index == 0) | (col_index == last_index), 0.5, 1.0)
     same = row_index == col_index
     denominator = jnp.where(same, 1.0, 2.0 * half_sum * half_diff)
     return jnp.where(same, 0.0, math.pi / last_index * sine_row * parity * weight / denominator)
 
 
-def parity_tables(points):
-    near, far = half_rows_of(points, False), half_rows_of(points, True)
-    near = near - jnp.diag(jnp.sum(near, axis=1) + jnp.sum(far, axis=1))
-    even, odd = near + far, near - far
-    second_even = jnp.dot(odd, even, precision=precise)
-    second_odd = jnp.dot(even, odd, precision=precise)
-    return even, odd, second_even, second_odd
+def fill_table(points, across, held, high_ref, low_ref):
+    half, step = points // 2, 16
+
+    def indices(chunk):
+        down = chunk * step + lax.broadcasted_iota(jnp.int32, (step, half), 0)
+        along = lax.broadcasted_iota(jnp.int32, (step, half), 1)
+        return (along, down) if across else (down, along)
+
+    def fill(chunk, total):
+        row, col = indices(chunk)
+        near, far = off_diagonal(points, row, col), off_diagonal(points, row, points - 1 - col)
+        even, odd = near + far, near - far
+        at = pl.ds(pl.multiple_of(chunk * step, step), step)
+        if not across:
+            own = jnp.where(row == col, jnp.sum(even, axis=1, keepdims=True), 0.0)
+            even, odd = even - own, odd - own
+        held[0, at, :] = even
+        held[1, at, :] = odd
+        return total + even
+
+    total = lax.fori_loop(0, half // step, fill, jnp.zeros((step, half), jnp.float32))
+    total = jnp.sum(total, axis=0, keepdims=True)
+
+    @pl.loop(0, half // step)
+    def _(chunk):
+        row, col = indices(chunk)
+        at = pl.ds(pl.multiple_of(chunk * step, step), step)
+        for k in range(2):
+            values = held[k, at, :]
+            if across:
+                values = values - jnp.where(row == col, total, 0.0)
+            high_ref[k, at, :], low_ref[k, at, :] = split2(values)
 
 
 def split2(x):
@@ -198,10 +219,14 @@
     return jnp.dot(a, b, preferred_element_type=jnp.float32)
 
 
-def dot3(a, b):
+def dot3(a, high, low):
     a_high, a_low = split2(a)
+    return mxu(a_high, high) + (mxu(a_high, low) + mxu(a_low, high))
+
+
+def dot3_left(high, low, b):
     b_high, b_low = split2(b)
-    return mxu(a_high, b_high) + (mxu(a_high, b_low) + mxu(a_low, b_high))
+    return mxu(high, b_high) + (mxu(low, b_high) + mxu(high, b_low))
 
 
 def exchange(size):
@@ -259,9 +284,10 @@
 
 
 def body(
-    groups, wave_ref, f_ref, c_ref, tz_ref, ty_ref, out_ref,
+    groups, wave_ref, f_ref, c_ref, out_ref,
+    held_z, high_z, low_z, held_y, high_y, low_y,
     pair, coef, far, far_coef, lines, line_coef, grad, curve, z_part, z_lines, whole, piece, outgoing,
-    local, cross_s, cross_r, coef_s, coef_r, own_s, own_r, fwd_s, fwd_r, lc_s, lc_r,
+    local, cross_s, cross_r, coef_s, coef_r, own_s, own_r, fwd_s, fwd_r, lc_s, lc_r, lm_s, lm_r,
     zp_s, zp_r, q_s, q_r, fin_s, fin_r,
 ):
     rows, cols = f_ref.shape[2], f_ref.shape[3]
@@ -303,6 +329,11 @@
 
     my_rows = pl.ds(pl.multiple_of(g * rows, rows), rows)
 
+    share = c_ref.shape[0] // 2
+    shared = pl.ds(core * share, share)
+    coef_cross = remote(
+        c_ref.at[shared], coef.at[h, shared], coef_s.at[0], coef_r.at[0], {"gz": 1 - h}
+    )
     cross = [
         remote(
             f_ref.at[1 - h, pl.ds(2 * k, 2)], pair.at[h, pl.ds(2 * k, 2)],
@@ -317,27 +348,51 @@
         )
         for d in range(1, groups)
     ]
-    share = c_ref.shape[0] // 2
-    shared = pl.ds(core * share, share)
-    coef_cross = remote(
-        c_ref.at[shared], coef.at[h, shared], coef_s.at[0], coef_r.at[0], {"gz": 1 - h}
-    )
     own_copy = here(f_ref.at[h], pair.at[h], 0)
     coef_copy = here(c_ref, coef.at[h], 1)
     line_copy = here(f_ref.at[h, :, :, block_of(h, g)], lines.at[h, :, my_rows, :], 2)
+    forwarded, line_copies = [], [line_copy]
+    fill_table(2 * cols, True, held_z, high_z, low_z)
+    fill_table(rows * groups, False, held_y, high_y, low_y)
+
+    coef_copy.wait()
+    coef_cross.wait_recv()
+    coef_mate = remote(
+        coef.at[1 - h, shared], coef.at[1 - h, shared], coef_s.at[1], coef_r.at[1], {"vec": 1 - core}
+    )
+    coef_mate.wait_recv()
+    coef_lines = []
+    for s in range(2):
+        for d in range(1, groups):
+            coef_lines.append(
+                remote(
+                    coef.at[s, 8 + core, :, block_of(s, peers[d])],
+                    line_coef.at[s, core, my_rows, :],
+                    lc_s.at[s, d], lc_r.at[s, d], {"gy": peers[d]},
+                )
+            )
+    coef_copies = [
+        here(coef.at[s, 8 + core, :, block_of(s, g)], line_coef.at[s, core, my_rows, :], 7 + s)
+        for s in range(2)
+    ]
+    for k in range(9):
+        far_coef[k] = flip_lanes(coef[1, k])
     own_copy.wait()
-    forwarded, line_copies = [], [line_copy]
 
     def derive(k):
         near = pair[0, 2 * k : 2 * k + 2].reshape(2 * rows, cols)
         mirror = flip_lanes(pair[1, 2 * k : 2 * k + 2].reshape(2 * rows, cols))
         far[2 * k : 2 * k + 2] = mirror.reshape(2, rows, cols)
         even, odd = 0.5 * (near + mirror), 0.5 * (near - mirror)
-        first, second = dot3(even, tz_ref[0]), dot3(odd, tz_ref[1])
+        first = dot3(even, high_z[0], low_z[0])
+        second = dot3(odd, high_z[1], low_z[1])
         grad[0, 2 * k : 2 * k + 2] = (second + first).reshape(2, rows, cols)
         grad[1, 2 * k : 2 * k + 2] = (second - first).reshape(2, rows, cols)
         if k < 3:
-            first, second = dot3(even, tz_ref[2]), dot3(odd, tz_ref[3])
+            first, second = (
+                dot3(first, high_z[1], low_z[1]),
+                dot3(second, high_z[0], low_z[0]),
+            )
             curve[0, 2 * k : 2 * k + 2] = (first + second).reshape(2, rows, cols)
             curve[1, 2 * k : 2 * k + 2] = (first - second).reshape(2, rows, cols)
 
@@ -361,27 +416,16 @@
         )
         derive(k)
 
-    coef_copy.wait()
-    coef_cross.wait_recv()
-    coef_mate = remote(
-        coef.at[1 - h, shared], coef.at[1 - h, shared], coef_s.at[1], coef_r.at[1], {"vec": 1 - core}
-    )
-    coef_mate.wait_recv()
-    coef_lines = []
-    for s in range(2):
-        for d in range(1, groups):
-            coef_lines.append(
-                remote(
-                    coef.at[s, pl.ds(8, 2), :, block_of(s, peers[d])],
-                    line_coef.at[s, :, my_rows, :],
-                    lc_s.at[s, d], lc_r.at[s, d], {"gy": peers[d]},
-                )
-            )
-        line_copies.append(
-            here(coef.at[s, pl.ds(8, 2), :, block_of(s, g)], line_coef.at[s, :, my_rows, :], 7 + s)
-        )
-    for k in range(9):
-        far_coef[k] = flip_lanes(coef[1, k])
+    for copy in coef_copies:
+        copy.wait()
+    for copy in coef_lines:
+        copy.wait_recv()
+    coef_mates = [
+        remote(
+            line_coef.at[s, core], line_coef.at[s, core], lm_s.at[s], lm_r.at[s], {"vec": 1 - core}
+        )
+        for s in range(2)
+    ]
 
     @pl.loop(0, rows // 8)
     def _(step):
@@ -401,18 +445,23 @@
         for k in range(4):
             z_part[2 * k : 2 * k + 2, at, :] = 0.5 * (near_action[k] + Z_SIGNS[k] * far_action[k])
 
-    z_moves = [
-        remote(
-            z_part.at[:, :, block(peers[d])], z_lines.at[:, my_rows, :],
-            zp_s.at[d], zp_r.at[d], {"gy": peers[d]},
-        )
-        for d in range(1, groups)
-    ]
-    z_copy = here(z_part.at[:, :, block(g)], z_lines.at[:, my_rows, :], 9)
+    z_moves, z_copies = [], []
+    for k in range(4):
+        two = pl.ds(2 * k, 2)
+        z_moves.append(
+            [
+                remote(
+                    z_part.at[two, :, block(peers[d])], z_lines.at[two, my_rows, :],
+                    zp_s.at[k, d], zp_r.at[k, d], {"gy": peers[d]},
+                )
+                for d in range(1, groups)
+            ]
+        )
+        z_copies.append(here(z_part.at[two, :, block(g)], z_lines.at[two, my_rows, :], 9 + k))
 
     for copy in line_copies:
         copy.wait()
-    for copy in own_lines + forwarded + coef_lines:
+    for copy in own_lines + forwarded + coef_mates:
         copy.wait_recv()
 
     def join(values):
@@ -444,10 +493,14 @@
             top = join(lines[s, 2 * k : 2 * k + 2, :half, :])
             bottom = flip_rows(join(lines[s, 2 * k : 2 * k + 2, half:, :]))
             even, odd = 0.5 * (top + bottom), 0.5 * (top - bottom)
-            first, second = dot3(ty_ref[0], even), dot3(ty_ref[1], odd)
+            first = dot3_left(high_y[0], low_y[0], even)
+            second = dot3_left(high_y[1], low_y[1], odd)
             grad_top, grad_low = second + first, second - first
             if k < 3:
-                first, second = dot3(ty_ref[2], even), dot3(ty_ref[3], odd)
+                first, second = (
+                    dot3_left(high_y[1], low_y[1], first),
+                    dot3_left(high_y[0], low_y[0], second),
+                )
                 top_action = top_advect * grad_top + top_nu * (first + second)
                 low_action = low_advect * grad_low + low_nu * (first - second)
                 add(k, 0.5 * (top_action + Y_SIGNS[k] * low_action), s == 0)
@@ -456,10 +509,31 @@
             if k == 3:
                 add(1, -0.5 * (grad_top + Y_SIGNS[1] * grad_low), False)
 
-    z_copy.wait()
-    for copy in z_moves:
-        copy.wait_recv()
+    results, finals = [], []
+
+    def finish(k):
+        two = slice(2 * k, 2 * k + 2)
+        for d in range(groups):
+            if d:
+                results[k][d - 1].wait_recv()
+            owner = lax.rem(g - d + groups, groups)
+            flat = (whole[two, my_rows, :] if d == 0 else piece[d, two]).reshape(2 * rows, width)
+            mirror = Z_SIGNS[k] * flip_lanes(flat)
+            flat, mirror = flat.reshape(2, rows, width), mirror.reshape(2, rows, width)
+            out_ref[h, two, :, block_of(h, owner)] = jnp.where(h == 0, flat, mirror)
+            outgoing[d, two] = jnp.where(h == 0, mirror, flat)
+            finals.append(
+                remote(
+                    outgoing.at[d, pl.ds(2 * k, 2)],
+                    out_ref.at[h, pl.ds(2 * k, 2), :, block_of(1 - h, owner)],
+                    fin_s.at[k, d], fin_r.at[k, d], {"gz": 1 - h},
+                )
+            )
+
     for k in range(4):
+        z_copies[k].wait()
+        for copy in z_moves[k]:
+            copy.wait_recv()
         top = join(z_lines[2 * k : 2 * k + 2, :half, :])
         bottom = flip_rows(join(z_lines[2 * k : 2 * k + 2, half:, :]))
         quarter = join(whole[2 * k : 2 * k + 2, :half, :]) + 0.5 * (top + Y_SIGNS[k] * bottom)
@@ -467,37 +541,25 @@
         for part in range(2):
             whole[2 * k + part, :half] = quarter[:, part * width : (part + 1) * width]
             whole[2 * k + part, half:] = mirror[:, part * width : (part + 1) * width]
-
-    results = [None]
-    for d in range(1, groups):
-        to_rows = pl.ds(pl.multiple_of(peers[d] * rows, rows), rows)
+        two = pl.ds(2 * k, 2)
         results.append(
-            remote(
-                whole.at[:, to_rows, :], piece.at[d], q_s.at[d], q_r.at[d], {"gy": peers[d]}
-            )
-        )
-    finals = []
-    for d in range(groups):
-        if d:
-            results[d].wait_recv()
-        owner = lax.rem(g - d + groups, groups)
-        flat = (whole[:, my_rows, :] if d == 0 else piece[d]).reshape(8 * rows, width)
-        mirror = flip_lanes(flat)
-        flat, mirror = flat.reshape(8, rows, width), mirror.reshape(8, rows, width)
-        mirror = jnp.concatenate((mirror[:4], -mirror[4:6], mirror[6:]))
-        out_ref[h, :, :, block_of(h, owner)] = jnp.where(h == 0, flat, mirror)
-        outgoing[d] = jnp.where(h == 0, mirror, flat)
-        finals.append(
-            remote(
-                outgoing.at[d], out_ref.at[h, :, :, block_of(1 - h, owner)],
-                fin_s.at[d], fin_r.at[d], {"gz": 1 - h},
-            )
-        )
+            [
+                remote(
+                    whole.at[two, pl.ds(pl.multiple_of(peers[d] * rows, rows), rows), :],
+                    piece.at[d, two],
+                    q_s.at[k, d], q_r.at[k, d], {"gy": peers[d]},
+                )
+                for d in range(1, groups)
+            ]
+        )
+        if k:
+            finish(k - 1)
+    finish(3)
     for copy in finals:
         copy.wait_recv()
-    for copy in cross + own_lines + [coef_cross, coef_mate] + forwarded + coef_lines + z_moves:
+    for copy in cross + own_lines + [coef_cross, coef_mate] + forwarded + coef_lines + coef_mates:
         copy.wait_send()
-    for copy in results[1:] + finals:
+    for copy in sum(z_moves, []) + sum(results, []) + finals:
         copy.wait_send()
 
 
@@ -513,18 +575,23 @@
             viscosity_slope[0:1] - mean_flow[1:2],
         )
     )
-    tables_z = jnp.stack([table.T for table in parity_tables(2 * cols)])
-    tables_y = jnp.stack(parity_tables(rows_total))
-    f32 = jnp.float32
+    f32, bf16 = jnp.float32, jnp.bfloat16
+    half = rows_total // 2
     dma = pltpu.SemaphoreType.DMA
     vmem = pl.BlockSpec(memory_space=pltpu.VMEM)
     anywhere = pl.BlockSpec(memory_space=pl.ANY)
     return pl.pallas_call(
         functools.partial(body, groups),
         out_shape=jax.ShapeDtypeStruct(forcing.shape, f32),
-        in_specs=[pl.BlockSpec(memory_space=pltpu.SMEM), anywhere, anywhere, vmem, vmem],
+        in_specs=[pl.BlockSpec(memory_space=pltpu.SMEM), anywhere, anywhere],
         out_specs=vmem,
         scratch_shapes=[
+            pltpu.VMEM((2, cols, cols), f32),
+            pltpu.VMEM((2, cols, cols), bf16),
+            pltpu.VMEM((2, cols, cols), bf16),
+            pltpu.VMEM((2, half, half), f32),
+            pltpu.VMEM((2, half, half), bf16),
+            pltpu.VMEM((2, half, half), bf16),
             pltpu.VMEM((2, 8, rows, cols), f32),
             pltpu.VMEM((2, 10, rows, cols), f32),
             pltpu.VMEM((8, rows, cols), f32),
@@ -538,20 +605,21 @@
             pltpu.VMEM((8, rows_total, width), f32),
             pltpu.VMEM((groups, 8, rows, width), f32),
             pltpu.VMEM((groups, 8, rows, width), f32),
-            dma((10,)),
+            dma((13,)),
             dma((4,)), dma((4,)),
             dma((2,)), dma((2,)),
             dma((groups,)), dma((groups,)),
             dma((4, groups)), dma((4, groups)),
             dma((2, groups)), dma((2, groups)),
-            dma((groups,)), dma((groups,)),
-            dma((groups,)), dma((groups,)),
-            dma((groups,)), dma((groups,)),
+            dma((2,)), dma((2,)),
+            dma((4, groups)), dma((4, groups)),
+            dma((4, groups)), dma((4, groups)),
+            dma((4, groups)), dma((4, groups)),
         ],
         compiler_params=pltpu.CompilerParams(
             collective_id=0, has_side_effects=True, vmem_limit_bytes=60 * 1024 * 1024
         ),
-    )(wavenumber, forcing, coefs, tables_z, tables_y)
+    )(wavenumber, forcing, coefs)
 
 
 def shards_of(mesh):

time: 287 us -> 226 us (0.79)
  Pallas kernels: 238 us -> 211 us
  matrix products: 23.2 us -> 0 us
  other arithmetic: 14.5 us -> 2.06 us
    pallas_call x1, Pallas kernels: 238 us -> 211 us  [paired_shards(): pl.pallas_call(functools.partial(body, groups), out_shape=jax.ShapeDtypeS...]
    dot_general x4 -> x0, matrix products: 23.2 us -> none  [the longest x2 11.6 us: parity_tables(): second_even = jnp.dot(odd, even, precision=precise)]
    reduce_sum x2 -> x0, other arithmetic: 6.04 us -> none  [parity_tables(): near = near - jnp.diag(jnp.sum(near, axis=1) + jnp.sum(far, axis=1))]
    add x4 -> x0, other arithmetic: 4.84 us -> none  [the longest x2 4.83 us: parity_tables(): even, odd = (near + far, near - far)]
    another operation x2 -> x0, other arithmetic: 3.5 us -> none  [the longest x1 2.46 us: paired_shards(): tables_z = jnp.stack([table.T for table in parity_tables(2 * cols)])]
    unnamed x12 -> x10, local copies, waits for them, and re-layouts: 7.29 us -> 8.9 us
where the time goes in v2:
time: 226 us; the launch traced here: 223 us
  Pallas kernels  211 us (93%)
  local copies, waits for them, and re-layouts  8.9 us (4%)
    pallas_call x1, Pallas kernels, paired_shards(): pl.pallas_call(functools.partial(body, groups), out_shape=jax.ShapeDtypeS...  211 us
    unnamed x10, local copies, waits for them, and re-layouts  8.9 us

profile of v2, /device:TPU:16, one launch (start us, length us, event | category | flops | bytes accessed | tf_op | source)
XLA Modules:
  0.0 223.0 jit_solution(7618652886810758341)
XLA Ops:
  0.0 0.0 copy-start.1
  0.0 0.0 copy-start.2
  0.7 1.0 slice_dynamic-update-slice_fusion.1
  1.7 1.1 subtract_dynamic-update-slice_fusion.1
  2.8 1.6 slice_dynamic-update-slice_fusion
  4.4 0.0 copy-done.2
  4.4 0.0 copy-done.1
  4.4 1.0 subtract_dynamic-update-slice_fusion.c_ref
  5.4 0.0 copy-start
  5.4 1.5 copy-done
  6.9 211.3 %shard_map.55 = f32[2,8,128,512]{3,2,1,0:T(8,128)} custom-call(f32[1]{0:T(128)S(6)} %copy.11.wave_ref, f32[2,8,128,512]{3,2,1,0:T(8,128)} %f_ref.1, f32[10,128,512]{2,1,0:T(8,128)} %copy-done), custom_call_target="tpu_custom_call" | custom-call | tf_op jit(solution)/shard_map/pallas_call | solution.py:583
  218.2 4.8 %copy.12 = f32[2,8,128,512]{3,2,1,0:T(8,128)} copy(f32[2,8,128,512]{3,2,1,0:T(8,128)} %shard_map.55) | data formatting | bytes 8388608
  (1 shorter events, 0.0 us)
Async XLA Ops:
  0.0 4.4 %copy-start.1 = (f32[2,128,512]{2,1,0:T(8,128)S(1)}, f32[2,128,512]{2,1,0:T(8,128)}, u32[]{:S(2)}) copy-start(f32[2,128,512]{2,1,0:T(8,128)} %param.9) | copy-start | bytes 1572868
  0.0 4.4 %copy-start.2 = (f32[128,512]{1,0:T(8,128)S(1)}, f32[128,512]{1,0:T(8,128)}, u32[]{:S(2)}) copy-start(f32[128,512]{1,0:T(8,128)} %param.8) | copy-start | bytes 786436
  5.4 1.5 copy-start

commit v3 on v2

--- a/solution.py
+++ b/solution.py
@@ -151,6 +151,7 @@
 
 Y_SIGNS = (1, -1, 1, 1)
 Z_SIGNS = (1, 1, -1, 1)
+Z_COEFS = (0, 11, 3, 4, 5, 6, 7, 8, 9)
 SINE_TERMS = 7
 
 
@@ -265,7 +266,7 @@
 
 def action_along_z(source, grad, curve, streamwise, coefs):
     u, v, w, p = source
-    stream, advect, uy, uz, vy, vz, wy, wz, nu = (coefs[k : k + 1] for k in range(9))
+    stream, advect, uy, uz, vy, vz, wy, wz, nu = (coefs[k : k + 1] for k in Z_COEFS)
     out = []
     for k, (c, sy, sz) in enumerate(((u, uy, uz), (v, vy, vz), (w, wy, wz))):
         term = (
@@ -284,9 +285,9 @@
 
 
 def body(
-    groups, wave_ref, f_ref, c_ref, out_ref,
+    groups, wave_ref, f_ref, flow_ref, nu_ref, slope_ref, out_ref,
     held_z, high_z, low_z, held_y, high_y, low_y,
-    pair, coef, far, far_coef, lines, line_coef, grad, curve, z_part, z_lines, whole, piece, outgoing,
+    pair, coef, far, far_coef, lines, line_coef, grad, curve, z_part, z_lines, whole, piece, kept, outgoing,
     local, cross_s, cross_r, coef_s, coef_r, own_s, own_r, fwd_s, fwd_r, lc_s, lc_r, lm_s, lm_r,
     zp_s, zp_r, q_s, q_r, fin_s, fin_r,
 ):
@@ -329,10 +330,23 @@
 
     my_rows = pl.ds(pl.multiple_of(g * rows, rows), rows)
 
-    share = c_ref.shape[0] // 2
-    shared = pl.ds(core * share, share)
+    own_lines = [
+        remote(
+            f_ref.at[h, :, :, block_of(h, peers[d])], lines.at[h, :, my_rows, :],
+            own_s.at[d], own_r.at[d], {"gy": peers[d]},
+        )
+        for d in range(1, groups)
+    ]
+    coef_copies = [
+        here(flow_ref, coef.at[h, pl.ds(0, 9)], 1),
+        here(nu_ref, coef.at[h, 9], 13),
+        here(slope_ref, coef.at[h, pl.ds(10, 2)], 14),
+    ]
+    for copy in coef_copies:
+        copy.wait()
+    shared = pl.ds(core * 6, 6)
     coef_cross = remote(
-        c_ref.at[shared], coef.at[h, shared], coef_s.at[0], coef_r.at[0], {"gz": 1 - h}
+        coef.at[h, shared], coef.at[h, shared], coef_s.at[0], coef_r.at[0], {"gz": 1 - h}
     )
     cross = [
         remote(
@@ -341,41 +355,37 @@
         )
         for k in range(4)
     ]
-    own_lines = [
-        remote(
-            f_ref.at[h, :, :, block_of(h, peers[d])], lines.at[h, :, my_rows, :],
-            own_s.at[d], own_r.at[d], {"gy": peers[d]},
-        )
-        for d in range(1, groups)
-    ]
     own_copy = here(f_ref.at[h], pair.at[h], 0)
-    coef_copy = here(c_ref, coef.at[h], 1)
     line_copy = here(f_ref.at[h, :, :, block_of(h, g)], lines.at[h, :, my_rows, :], 2)
     forwarded, line_copies = [], [line_copy]
     fill_table(2 * cols, True, held_z, high_z, low_z)
     fill_table(rows * groups, False, held_y, high_y, low_y)
 
-    coef_copy.wait()
     coef_cross.wait_recv()
     coef_mate = remote(
         coef.at[1 - h, shared], coef.at[1 - h, shared], coef_s.at[1], coef_r.at[1], {"vec": 1 - core}
     )
     coef_mate.wait_recv()
+    coef_cross.wait_send()
+    coef_mate.wait_send()
+    for s in range(2):
+        for k in range(2):
+            coef[s, 10 + k] = coef[s, 10 + k] - coef[s, 1 + k]
     coef_lines = []
     for s in range(2):
         for d in range(1, groups):
             coef_lines.append(
                 remote(
-                    coef.at[s, 8 + core, :, block_of(s, peers[d])],
+                    coef.at[s, 9 + core, :, block_of(s, peers[d])],
                     line_coef.at[s, core, my_rows, :],
                     lc_s.at[s, d], lc_r.at[s, d], {"gy": peers[d]},
                 )
             )
     coef_copies = [
-        here(coef.at[s, 8 + core, :, block_of(s, g)], line_coef.at[s, core, my_rows, :], 7 + s)
+        here(coef.at[s, 9 + core, :, block_of(s, g)], line_coef.at[s, core, my_rows, :], 7 + s)
         for s in range(2)
     ]
-    for k in range(9):
+    for k in Z_COEFS:
         far_coef[k] = flip_lanes(coef[1, k])
     own_copy.wait()
 
@@ -440,8 +450,8 @@
                 coefs,
             )
 
-        near_action = act(pair.at[0], 0, coef[0, 0:9, at, :])
-        far_action = act(far, 1, far_coef[0:9, at, :])
+        near_action = act(pair.at[0], 0, coef[0, :, at, :])
+        far_action = act(far, 1, far_coef[:, at, :])
         for k in range(4):
             z_part[2 * k : 2 * k + 2, at, :] = 0.5 * (near_action[k] + Z_SIGNS[k] * far_action[k])
 
@@ -509,26 +519,25 @@
             if k == 3:
                 add(1, -0.5 * (grad_top + Y_SIGNS[1] * grad_low), False)
 
-    results, finals = [], []
+    results, finals, stored = [], [], []
 
     def finish(k):
-        two = slice(2 * k, 2 * k + 2)
-        for d in range(groups):
-            if d:
-                results[k][d - 1].wait_recv()
-            owner = lax.rem(g - d + groups, groups)
-            flat = (whole[two, my_rows, :] if d == 0 else piece[d, two]).reshape(2 * rows, width)
-            mirror = Z_SIGNS[k] * flip_lanes(flat)
-            flat, mirror = flat.reshape(2, rows, width), mirror.reshape(2, rows, width)
-            out_ref[h, two, :, block_of(h, owner)] = jnp.where(h == 0, flat, mirror)
-            outgoing[d, two] = jnp.where(h == 0, mirror, flat)
-            finals.append(
-                remote(
-                    outgoing.at[d, pl.ds(2 * k, 2)],
-                    out_ref.at[h, pl.ds(2 * k, 2), :, block_of(1 - h, owner)],
-                    fin_s.at[k, d], fin_r.at[k, d], {"gz": 1 - h},
+        for c in (2 * k, 2 * k + 1):
+            for d in range(groups):
+                if d:
+                    results[c][d - 1].wait_recv()
+                owner = lax.rem(g - d + groups, groups)
+                flat = whole[c, my_rows, :] if d == 0 else piece[d, c]
+                mirror = Z_SIGNS[k] * flip_lanes(flat)
+                kept[c, :, block_of(h, owner)] = jnp.where(h == 0, flat, mirror)
+                outgoing[d, c] = jnp.where(h == 0, mirror, flat)
+                finals.append(
+                    remote(
+                        outgoing.at[d, c], out_ref.at[h, c, :, block_of(1 - h, owner)],
+                        fin_s.at[c, d], fin_r.at[c, d], {"gz": 1 - h},
+                    )
                 )
-            )
+            stored.append(here(kept.at[c], out_ref.at[h, c], 15 + c))
 
     for k in range(4):
         z_copies[k].wait()
@@ -541,23 +550,25 @@
         for part in range(2):
             whole[2 * k + part, :half] = quarter[:, part * width : (part + 1) * width]
             whole[2 * k + part, half:] = mirror[:, part * width : (part + 1) * width]
-        two = pl.ds(2 * k, 2)
-        results.append(
-            [
-                remote(
-                    whole.at[two, pl.ds(pl.multiple_of(peers[d] * rows, rows), rows), :],
-                    piece.at[d, two],
-                    q_s.at[k, d], q_r.at[k, d], {"gy": peers[d]},
-                )
-                for d in range(1, groups)
-            ]
-        )
+        for c in (2 * k, 2 * k + 1):
+            results.append(
+                [
+                    remote(
+                        whole.at[c, pl.ds(pl.multiple_of(peers[d] * rows, rows), rows), :],
+                        piece.at[d, c],
+                        q_s.at[c, d], q_r.at[c, d], {"gy": peers[d]},
+                    )
+                    for d in range(1, groups)
+                ]
+            )
         if k:
             finish(k - 1)
     finish(3)
+    for copy in stored:
+        copy.wait()
     for copy in finals:
         copy.wait_recv()
-    for copy in cross + own_lines + [coef_cross, coef_mate] + forwarded + coef_lines + coef_mates:
+    for copy in cross + own_lines + forwarded + coef_lines + coef_mates:
         copy.wait_send()
     for copy in sum(z_moves, []) + sum(results, []) + finals:
         copy.wait_send()
@@ -566,25 +577,15 @@
 def paired_shards(groups, forcing, wavenumber, mean_flow, viscosity, viscosity_slope):
     vectors, components, rows, cols = forcing.shape
     width, rows_total = cols // groups, rows * groups
-    coefs = jnp.concatenate(
-        (
-            mean_flow[0:1],
-            viscosity_slope[1:2] - mean_flow[2:3],
-            mean_flow[3:9],
-            viscosity[None],
-            viscosity_slope[0:1] - mean_flow[1:2],
-        )
-    )
     f32, bf16 = jnp.float32, jnp.bfloat16
     half = rows_total // 2
     dma = pltpu.SemaphoreType.DMA
-    vmem = pl.BlockSpec(memory_space=pltpu.VMEM)
     anywhere = pl.BlockSpec(memory_space=pl.ANY)
     return pl.pallas_call(
         functools.partial(body, groups),
         out_shape=jax.ShapeDtypeStruct(forcing.shape, f32),
-        in_specs=[pl.BlockSpec(memory_space=pltpu.SMEM), anywhere, anywhere],
-        out_specs=vmem,
+        in_specs=[pl.BlockSpec(memory_space=pltpu.SMEM), anywhere, anywhere, anywhere, anywhere],
+        out_specs=anywhere,
         scratch_shapes=[
             pltpu.VMEM((2, cols, cols), f32),
             pltpu.VMEM((2, cols, cols), bf16),
@@ -593,9 +594,9 @@
             pltpu.VMEM((2, half, half), bf16),
             pltpu.VMEM((2, half, half), bf16),
             pltpu.VMEM((2, 8, rows, cols), f32),
-            pltpu.VMEM((2, 10, rows, cols), f32),
+            pltpu.VMEM((2, 12, rows, cols), f32),
             pltpu.VMEM((8, rows, cols), f32),
-            pltpu.VMEM((9, rows, cols), f32),
+            pltpu.VMEM((12, rows, cols), f32),
             pltpu.VMEM((2, 8, rows_total, width), f32),
             pltpu.VMEM((2, 2, rows_total, width), f32),
             pltpu.VMEM((2, 8, rows, cols), f32),
@@ -604,8 +605,9 @@
             pltpu.VMEM((8, rows_total, width), f32),
             pltpu.VMEM((8, rows_total, width), f32),
             pltpu.VMEM((groups, 8, rows, width), f32),
+            pltpu.VMEM((8, rows, cols), f32),
             pltpu.VMEM((groups, 8, rows, width), f32),
-            dma((13,)),
+            dma((23,)),
             dma((4,)), dma((4,)),
             dma((2,)), dma((2,)),
             dma((groups,)), dma((groups,)),
@@ -613,13 +615,13 @@
             dma((2, groups)), dma((2, groups)),
             dma((2,)), dma((2,)),
             dma((4, groups)), dma((4, groups)),
-            dma((4, groups)), dma((4, groups)),
-            dma((4, groups)), dma((4, groups)),
+            dma((8, groups)), dma((8, groups)),
+            dma((8, groups)), dma((8, groups)),
         ],
         compiler_params=pltpu.CompilerParams(
             collective_id=0, has_side_effects=True, vmem_limit_bytes=60 * 1024 * 1024
         ),
-    )(wavenumber, forcing, coefs)
+    )(wavenumber, forcing, mean_flow, viscosity, viscosity_slope)
 
 
 def shards_of(mesh):

time: 226 us -> 217 us (0.960)
  local copies, waits for them, and re-layouts: 8.9 us -> 4.81 us
    unnamed x10 -> x1, local copies, waits for them, and re-layouts: 8.9 us -> 4.81 us
where the time goes in v3:
time: 217 us; the launch traced here: 216 us
  Pallas kernels  210 us (97%)
  local copies, waits for them, and re-layouts  4.81 us (2%)
    pallas_call x1, Pallas kernels, paired_shards(): pl.pallas_call(functools.partial(body, groups), out_shape=jax.ShapeDtypeS...  210 us
    unnamed x1, local copies, waits for them, and re-layouts  4.81 us

profile of v3, /device:TPU:16, one launch (start us, length us, event | category | flops | bytes accessed | tf_op | source)
XLA Modules:
  0.0 215.6 jit_solution(5643084519300797628)
XLA Ops:
  0.7 210.2 %shard_map.55 = f32[2,8,128,512]{3,2,1,0:T(8,128)} custom-call(f32[1]{0:T(128)S(6)} %copy.7.wave_ref, f32[2,8,128,512]{3,2,1,0:T(8,128)} %f_ref.1, f32[9,128,512]{2,1,0:T(8,128)} %flow_ref.1, f32[128,512]{1,0:T(8,128)} %nu_ref.1, f32[2,128,512]{2,1,0:T(8,128)} %slope_ref.1), custom_call_target="tpu_custom_call" | custom-call | tf_op jit(solution)/shard_map/pallas_call | solution.py:584
  210.8 4.8 %copy.8 = f32[2,8,128,512]{3,2,1,0:T(8,128)} copy(f32[2,8,128,512]{3,2,1,0:T(8,128)} %shard_map.55) | data formatting | bytes 8388608
